TPU v7x, 32 devices: a whole 2x2x4 slice. The times are simulated.
32 devices in a mesh: gx: 4 (over y, x), gy: 2 (over core), gz: 4 (over z).
Axes of the slice: x: 2, y: 2, z: 4, core: 2. Of those that a mesh axis runs over, the one named last changes fastest.
Arguments:
- flexibility: bfloat16 [4, 2, 4, 768, 768], P('gx', 'gy', 'gz'), may hold values from -6 to 6, as said below
- stiffness: bfloat16 [4, 2, 4, 768, 768], P('gx', 'gy', 'gz'), may hold values from -6 to 6, as said below
- local_load: float32 [4, 2, 4, 6, 128, 128], P('gx', 'gy', 'gz'), may hold values from -80 to 80
- face_map: int32 [4, 2, 4, 6, 128], P('gx', 'gy', 'gz'), may hold values from 0 to 127, each once within a row
- face_sign: int32 [4, 2, 4, 6, 128], P('gx', 'gy', 'gz'), may hold values from -1 to 1, as said below
Outputs:
- multipliers: float32 [4, 2, 4, 3, 128, 128], P('gx', 'gy', 'gz')
- residual: float32 [4, 2, 4, 3, 128, 128], P('gx', 'gy', 'gz')
Inputs may be any that keep to these rules, and one draw needn't show every extreme that they name: `face_map`: each row is a permutation of 0 to 127. `face_sign`: every entry is +1 or -1, and the two subdomains sharing a face give each of its multipliers opposite signs. `flexibility`: each subdomain's matrix is symmetric positive definite. `stiffness`: each subdomain's matrix is symmetric positive definite.
All inputs are finite; a program needn't handle non-finite values.
Results may differ from a plain program's by a relative error of at most 0.011.
Values sent between devices are 32-bit elements; how exact they have to be, the bound alone decides.
A program may use at most 64 MiB of HBM per device.

v0:
```python
import jax
import jax.numpy as jnp
from jax import lax
from jax.sharding import PartitionSpec as P

ITERS = 2


def with_halo(array, sides, width):
    for axis, dim in sides:
        count, length = (lax.axis_size(axis), array.shape[dim])
        up = [(i, (i + 1) % count) for i in range(count)]
        down = [(j, i) for i, j in up]
        last = lax.slice_in_dim(array, length - width, length, axis=dim)
        first = lax.slice_in_dim(array, 0, width, axis=dim)
        before = lax.ppermute(last, axis, up)
        after = lax.ppermute(first, axis, down)
        array = jnp.concatenate([before, array, after], axis=dim)
    return array


def assemble(vector):
    along_x = with_halo(vector[0:2], (("gx", 0),), 1)
    along_y = with_halo(vector[2:4], (("gy", 0),), 1)
    along_z = with_halo(vector[4:6], (("gz", 0),), 1)
    return jnp.stack(
        [
            vector[0] + along_x[0],
            vector[1] + along_x[3],
            vector[2] + along_y[0],
            vector[3] + along_y[3],
            vector[4] + along_z[0],
            vector[5] + along_z[3],
        ]
    )


def local_product(operator, face_rows, inverse, signs, vector):
    width = vector.shape[1]
    columns = vector.shape[2]
    signed = (signs * vector).reshape(6 * width, columns)
    restricted = signed[inverse].astype(jnp.bfloat16)
    product = jnp.dot(operator, restricted, preferred_element_type=jnp.float32)
    return signs * product[face_rows].reshape(6, width, columns)


def apply_operator(operator, face_rows, inverse, signs, vector):
    return assemble(local_product(operator, face_rows, inverse, signs, vector))


def inner_pair(residual, precond, image_z):
    gamma_part = jnp.sum(residual[0::2] * precond[0::2], axis=(0, 1))
    delta_part = jnp.sum(precond[0::2] * image_z[0::2], axis=(0, 1))
    return lax.psum((gamma_part, delta_part), ("gx", "gy", "gz"))


def shards(flexibility, stiffness, local_load, face_map, face_sign):
    flex_local = flexibility[0, 0, 0]
    stiff_local = stiffness[0, 0, 0]
    width = face_map.shape[-1]
    maps_local = face_map[0, 0, 0]
    signs = face_sign[0, 0, 0].astype(jnp.float32)[:, :, None]
    face_rows = (jnp.arange(6, dtype=jnp.int32)[:, None] * width + maps_local).reshape(-1)
    inverse = (
        jnp.zeros((6 * width,), jnp.int32).at[face_rows].set(jnp.arange(6 * width, dtype=jnp.int32))
    )
    residual = assemble(local_load[0, 0, 0])
    multipliers = jnp.zeros_like(residual)
    precond = apply_operator(stiff_local, face_rows, inverse, signs, residual)
    image_z = apply_operator(flex_local, face_rows, inverse, signs, precond)
    gamma_now, delta_now = inner_pair(residual, precond, image_z)
    step_size = gamma_now / delta_now
    direction = precond
    image_dir = image_z
    for iteration in range(ITERS):
        multipliers = multipliers + step_size * direction
        residual = residual - step_size * image_dir
        if iteration + 1 < ITERS:
            precond = apply_operator(stiff_local, face_rows, inverse, signs, residual)
            image_z = apply_operator(flex_local, face_rows, inverse, signs, precond)
            gamma_new, delta_now = inner_pair(residual, precond, image_z)
            conjugacy = gamma_new / gamma_now
            step_size = gamma_new / (delta_now - conjugacy * gamma_new / step_size)
            direction = precond + conjugacy * direction
            image_dir = image_z + conjugacy * image_dir
            gamma_now = gamma_new
    return (multipliers[0::2][None, None, None], residual[0::2][None, None, None])


def solution(mesh):
    in_specs = (
        P("gx", "gy", "gz", None, None),
        P("gx", "gy", "gz", None, None),
        P("gx", "gy", "gz", None, None, None),
        P("gx", "gy", "gz", None, None),
        P("gx", "gy", "gz", None, None),
    )
    out_specs = (P("gx", "gy", "gz", None, None, None), P("gx", "gy", "gz", None, None, None))
    return jax.shard_map(shards, mesh=mesh, in_specs=in_specs, out_specs=out_specs, check_vma=False)
```

profile of v0, /device:TPU:0, one launch (start us, length us, event | category | flops | bytes accessed | tf_op | source)
XLA Modules:
  0.0 179.2 jit_solution(13809271839440472968)
XLA Ops:
  0.7 1.1 slice_bitcast_fusion.3
  1.8 5.1 %collective-permute-start.5 = (f32[1,128,128]{2,1,0:T(8,128)S(1)}, f32[1,128,128]{2,1,0:T(8,128)S(1)}, u32[]{:S(2)}, u32[]{:S(2)}) collective-permute-start(f32[1,128,128]{2,1,0:T(8,128)S(1)} %get-tuple-element.36), channel_id=1, source_target_pairs={{1,0},{2,1},{3,2},{0,3},{5,4},{6,5},{7,6},{4,7},{9,8},{10,9},{11,1... | collective-permute-start | bytes 196616 | tf_op jit(solution)/shard_map/ppermute | solution.py:17
  7.4 1.5 collective-permute-start
  8.9 1.4 collective-permute-start.1
  12.5 3.4 %scatter_custom_fusion = s32[768]{0:T(1024)S(1)} fusion(s32[768]{0:T(1024)S(1)} %fusion.10, s32[768]{0:T(1024)S(1)} %iota.9, s32[]{:T(128)} %constant.0.clone.1), kind=kCustom, calls=%fused_computation.84 | custom fusion | bytes 3076 | tf_op jit(solution)/shard_map/scatter | solution.py:65
  16.0 0.9 add_dynamic-update-slice_fusion.29
  16.9 0.9 add_dynamic-update-slice_fusion.28
  17.8 4.3 %collective-permute-done.4 = f32[1,128,128]{2,1,0:T(8,128)S(1)} collective-permute-done((f32[1,128,128]{2,1,0:T(8,128)S(1)}, f32[1,128,128]{2,1,0:T(8,128)S(1)}, u32[]{:S(2)}, u32[]{:S(2)}) %collective-permute-start.4) | collective-permute-done | bytes 65568 | tf_op jit(solution)/shard_map/ppermute | solution.py:16
  22.3 1.9 %gather_fusion = bf16[768,128]{1,0:T(8,128)(2,1)S(1)} fusion(bf16[768,128]{1,0:T(8,128)(2,1)S(1)} %bitcast_multiply_fusion.3, s32[1024]{0:T(1024)S(1)} %pad_clamp_fusion.1), kind=kCustom, calls=%fused_computation | custom fusion | bytes 396288 | tf_op jit(solution)/shard_map/gather | solution.py:42
  24.9 1.6 gather_fusion.1
  27.3 4.6 %collective-permute-done.6 = f32[1,128,128]{2,1,0:T(8,128)S(1)} collective-permute-done((f32[1,128,128]{2,1,0:T(8,128)S(1)}, f32[1,128,128]{2,1,0:T(8,128)S(1)}, u32[]{:S(2)}, u32[]{:S(2)}) %collective-permute-start.6) | collective-permute-done | bytes 65568 | tf_op jit(solution)/shard_map/ppermute | solution.py:16
  32.6 2.0 %collective-permute-start.10 = (f32[1,128,128]{2,1,0:T(8,128)S(1)}, f32[1,128,128]{2,1,0:T(8,128)S(1)}, u32[]{:S(2)}, u32[]{:S(2)}) collective-permute-start(f32[1,128,128]{2,1,0:T(8,128)S(1)} %get-tuple-element.32), channel_id=1, source_target_pairs={{0,1},{1,2},{2,3},{3,0},{4,5},{5,6},{6,7},{7,4},{8,9},{9,10},{10,1... | collective-permute-start | bytes 196616 | tf_op jit(solution)/shard_map/ppermute | solution.py:16
  35.1 1.1 collective-permute-done.7
  36.3 2.4 %collective-permute-done.10 = f32[1,128,128]{2,1,0:T(8,128)S(1)} collective-permute-done((f32[1,128,128]{2,1,0:T(8,128)S(1)}, f32[1,128,128]{2,1,0:T(8,128)S(1)}, u32[]{:S(2)}, u32[]{:S(2)}) %collective-permute-start.10) | collective-permute-done | bytes 65568 | tf_op jit(solution)/shard_map/ppermute | solution.py:16
  38.9 1.9 %gather_fusion.2 = bf16[768,128]{1,0:T(8,128)(2,1)S(1)} fusion(bf16[768,128]{1,0:T(8,128)(2,1)S(1)} %bitcast_multiply_fusion.2, s32[1024]{0:T(1024)S(1)} %pad_clamp_fusion.1), kind=kCustom, calls=%fused_computation.2 | custom fusion | bytes 396288 | tf_op jit(solution)/shard_map/gather | solution.py:42
  40.8 1.3 convolution_bitcast_fusion.2
  42.1 1.1 copy.8
  43.3 1.6 gather_fusion.3
  45.0 1.4 collective-permute-start.12
  46.5 3.9 %collective-permute-done.12 = f32[1,128,128]{2,1,0:T(8,128)S(1)} collective-permute-done((f32[1,128,128]{2,1,0:T(8,128)S(1)}, f32[1,128,128]{2,1,0:T(8,128)S(1)}, u32[]{:S(2)}, u32[]{:S(2)}) %collective-permute-start.12) | collective-permute-done | bytes 65568 | tf_op jit(solution)/shard_map/ppermute | solution.py:16
  50.4 2.0 %collective-permute-start.13 = (f32[1,128,128]{2,1,0:T(8,128)S(1)}, f32[1,128,128]{2,1,0:T(8,128)S(1)}, u32[]{:S(2)}, u32[]{:S(2)}) collective-permute-start(f32[1,128,128]{2,1,0:T(8,128)S(1)} %get-tuple-element.29), channel_id=1, source_target_pairs={{8,0},{16,8},{24,16},{0,24},{9,1},{17,9},{25,17},{1,25},{10,2},{18... | collective-permute-start | bytes 196616 | tf_op jit(solution)/shard_map/ppermute | solution.py:17
  52.4 2.0 %collective-permute-start.16 = (f32[1,128,128]{2,1,0:T(8,128)S(1)}, f32[1,128,128]{2,1,0:T(8,128)S(1)}, u32[]{:S(2)}, u32[]{:S(2)}) collective-permute-start(f32[1,128,128]{2,1,0:T(8,128)S(1)} %get-tuple-element.26), channel_id=1, source_target_pairs={{0,1},{1,2},{2,3},{3,0},{4,5},{5,6},{6,7},{7,4},{8,9},{9,10},{10,1... | collective-permute-start | bytes 196616 | tf_op jit(solution)/shard_map/ppermute | solution.py:16
  55.0 0.7 collective-permute-done.14
  55.9 2.6 %collective-permute-done.16 = f32[1,128,128]{2,1,0:T(8,128)S(1)} collective-permute-done((f32[1,128,128]{2,1,0:T(8,128)S(1)}, f32[1,128,128]{2,1,0:T(8,128)S(1)}, u32[]{:S(2)}, u32[]{:S(2)}) %collective-permute-start.16) | collective-permute-done | bytes 65568 | tf_op jit(solution)/shard_map/ppermute | solution.py:16
  58.6 38.0 %all-reduce.1 = (f32[128]{0:T(128)S(1)}, f32[128]{0:T(128)S(1)}) all-reduce(f32[128]{0:T(128)S(1)} %get-tuple-element.5, f32[128]{0:T(128)S(1)} %get-tuple-element.4), channel_id=1, replica_groups=mesh['gx'=4,'gy'=2,'gz'=4] {'gx','gy','gz'}, use_global_device_ids=true, to_apply=%region_2.0 | all-reduce | flops 256 | bytes 2048 | tf_op jit(solution)/shard_map/psum | solution.py:54
  97.8 1.9 %gather_fusion.4 = bf16[768,128]{1,0:T(8,128)(2,1)S(1)} fusion(bf16[768,128]{1,0:T(8,128)(2,1)S(1)} %fusion.5, s32[1024]{0:T(1024)S(1)} %pad_clamp_fusion.1), kind=kCustom, calls=%fused_computation.4 | custom fusion | bytes 396288 | tf_op jit(solution)/shard_map/gather | solution.py:42
  99.7 1.3 convolution_bitcast_fusion.1
  101.0 1.1 copy.9
  102.2 2.3 %gather_fusion.5 = f32[768,128]{1,0:T(8,128)} fusion(f32[768,128]{1,0:T(8,128)S(1)} %copy.9, s32[1024]{0:T(1024)S(1)} %pad_clamp_fusion), kind=kCustom, calls=%fused_computation.5 | custom fusion | bytes 789504 | tf_op jit(solution)/shard_map/gather | solution.py:44
  104.5 1.2 broadcast_multiply_fusion.1
  105.6 2.3 %collective-permute-start.18 = (f32[1,128,128]{2,1,0:T(8,128)S(1)}, f32[1,128,128]{2,1,0:T(8,128)S(1)}, u32[]{:S(2)}, u32[]{:S(2)}) collective-permute-start(f32[1,128,128]{2,1,0:T(8,128)S(1)} %slice.282), channel_id=1, source_target_pairs={{0,8},{8,16},{16,24},{24,0},{1,9},{9,17},{17,25},{25,1},{2,10},{10... | collective-permute-start | bytes 196616 | tf_op jit(solution)/shard_map/ppermute | solution.py:16
  108.0 2.9 %collective-permute-done.18 = f32[1,128,128]{2,1,0:T(8,128)S(1)} collective-permute-done((f32[1,128,128]{2,1,0:T(8,128)S(1)}, f32[1,128,128]{2,1,0:T(8,128)S(1)}, u32[]{:S(2)}, u32[]{:S(2)}) %collective-permute-start.18) | collective-permute-done | bytes 65568 | tf_op jit(solution)/shard_map/ppermute | solution.py:16
  110.9 1.0 collective-permute-start.19
  111.9 1.6 collective-permute-start.23
  114.4 0.8 collective-permute-done.19
  115.3 4.2 %collective-permute-done.22 = f32[1,128,128]{2,1,0:T(8,128)S(1)} collective-permute-done((f32[1,128,128]{2,1,0:T(8,128)S(1)}, f32[1,128,128]{2,1,0:T(8,128)S(1)}, u32[]{:S(2)}, u32[]{:S(2)}) %collective-permute-start.22) | collective-permute-done | bytes 65568 | tf_op jit(solution)/shard_map/ppermute | solution.py:16
  119.6 0.8 copy-done.5
  120.5 2.5 %gather_fusion.6 = bf16[768,128]{1,0:T(8,128)(2,1)} fusion(bf16[768,128]{1,0:T(8,128)(2,1)S(1)} %bitcast_multiply_fusion, s32[1024]{0:T(1024)S(1)} %pad_clamp_fusion.1), kind=kCustom, calls=%fused_computation.6 | custom fusion | bytes 396288 | tf_op jit(solution)/shard_map/gather | solution.py:42
  123.0 1.5 convolution_bitcast_fusion
  124.7 1.6 gather_fusion.7
  126.4 1.1 collective-permute-start.24
  127.5 4.6 %collective-permute-done.24 = f32[1,128,128]{2,1,0:T(8,128)S(1)} collective-permute-done((f32[1,128,128]{2,1,0:T(8,128)S(1)}, f32[1,128,128]{2,1,0:T(8,128)S(1)}, u32[]{:S(2)}, u32[]{:S(2)}) %collective-permute-start.24) | collective-permute-done | bytes 65568 | tf_op jit(solution)/shard_map/ppermute | solution.py:16
  132.2 1.7 collective-permute-start.25
  134.0 1.0 collective-permute-start.29
  135.0 1.1 collective-permute-start.28
  137.5 3.5 %collective-permute-done.28 = f32[1,128,128]{2,1,0:T(8,128)S(1)} collective-permute-done((f32[1,128,128]{2,1,0:T(8,128)S(1)}, f32[1,128,128]{2,1,0:T(8,128)S(1)}, u32[]{:S(2)}, u32[]{:S(2)}) %collective-permute-start.28) | collective-permute-done | bytes 65568 | tf_op jit(solution)/shard_map/ppermute | solution.py:16
  141.2 37.0 %all-reduce = (f32[128]{0:T(128)S(1)}, f32[128]{0:T(128)S(1)}) all-reduce(f32[128]{0:T(128)S(1)} %get-tuple-element.3, f32[128]{0:T(128)S(1)} %get-tuple-element.2), channel_id=1, replica_groups=mesh['gx'=4,'gy'=2,'gz'=4] {'gx','gy','gz'}, use_global_device_ids=true, to_apply=%region_6.0 | all-reduce | flops 256 | bytes 2048 | tf_op jit(solution)/shard_map/psum | solution.py:54
  178.4 0.8 slice_bitcast_fusion
  (119 shorter events, 11.6 us)
Async XLA Ops:
  0.6 23.6 %copy-start = (bf16[1,1,1,768,768]{4,3,2,1,0:T(8,128)(2,1)S(1)}, bf16[1,1,1,768,768]{4,3,2,1,0:T(8,128)(2,1)}, u32[]{:S(2)}) copy-start(bf16[1,1,1,768,768]{4,3,2,1,0:T(8,128)(2,1)} %param.6) | copy-start | bytes 3538948
  0.6 17.1 %copy-start.7 = (f32[1,1,1,6,128,128]{5,4,3,2,1,0:T(8,128)S(1)}, f32[1,1,1,6,128,128]{5,4,3,2,1,0:T(8,128)}, u32[]{:S(2)}) copy-start(f32[1,1,1,6,128,128]{5,4,3,2,1,0:T(8,128)} %param.7) | copy-start | bytes 1179652
  1.8 20.3 %collective-permute-start.5 = (f32[1,128,128]{2,1,0:T(8,128)S(1)}, f32[1,128,128]{2,1,0:T(8,128)S(1)}, u32[]{:S(2)}, u32[]{:S(2)}) collective-permute-start(f32[1,128,128]{2,1,0:T(8,128)S(1)} %get-tuple-element.36), channel_id=1, source_target_pairs={{1,0},{2,1},{3,2},{0,3},{5,4},{6,5},{7,6},{4,7},{9,8},{10,9},{11,1... | collective-permute-start | bytes 196616 | tf_op jit(solution)/shard_map/ppermute | solution.py:17
  6.9 10.8 %collective-permute-start.2 = (f32[1,128,128]{2,1,0:T(8,128)S(1)}, f32[1,128,128]{2,1,0:T(8,128)S(1)}, u32[]{:S(2)}, u32[]{:S(2)}) collective-permute-start(f32[1,128,128]{2,1,0:T(8,128)S(1)} %get-tuple-element.37), channel_id=1, source_target_pairs={{0,4},{4,0},{1,5},{5,1},{2,6},{6,2},{3,7},{7,3},{8,12},{12,8},{9,1... | collective-permute-start | bytes 196616 | tf_op jit(solution)/shard_map/ppermute | solution.py:16
  6.9 10.9 %collective-permute-start.3 = (f32[1,128,128]{2,1,0:T(8,128)S(1)}, f32[1,128,128]{2,1,0:T(8,128)S(1)}, u32[]{:S(2)}, u32[]{:S(2)}) collective-permute-start(f32[1,128,128]{2,1,0:T(8,128)S(1)} %get-tuple-element.38), channel_id=1, source_target_pairs={{4,0},{0,4},{5,1},{1,5},{6,2},{2,6},{7,3},{3,7},{12,8},{8,12},{13,... | collective-permute-start | bytes 196616 | tf_op jit(solution)/shard_map/ppermute | solution.py:17
  7.4 8.5 %collective-permute-start = (f32[1,128,128]{2,1,0:T(8,128)S(1)}, f32[1,128,128]{2,1,0:T(8,128)S(1)}, u32[]{:S(2)}, u32[]{:S(2)}) collective-permute-start(f32[1,128,128]{2,1,0:T(8,128)S(1)} %get-tuple-element.39), channel_id=1, source_target_pairs={{0,8},{8,16},{16,24},{24,0},{1,9},{9,17},{17,25},{25,1},{2,10},{10... | collective-permute-start | bytes 196616 | tf_op jit(solution)/shard_map/ppermute | solution.py:16
  8.9 8.0 %collective-permute-start.1 = (f32[1,128,128]{2,1,0:T(8,128)S(1)}, f32[1,128,128]{2,1,0:T(8,128)S(1)}, u32[]{:S(2)}, u32[]{:S(2)}) collective-permute-start(f32[1,128,128]{2,1,0:T(8,128)S(1)} %get-tuple-element.40), channel_id=1, source_target_pairs={{8,0},{16,8},{24,16},{0,24},{9,1},{17,9},{25,17},{1,25},{10,2},{18... | collective-permute-start | bytes 196616 | tf_op jit(solution)/shard_map/ppermute | solution.py:17
  16.0 6.1 %collective-permute-start.4 = (f32[1,128,128]{2,1,0:T(8,128)S(1)}, f32[1,128,128]{2,1,0:T(8,128)S(1)}, u32[]{:S(2)}, u32[]{:S(2)}) collective-permute-start(f32[1,128,128]{2,1,0:T(8,128)S(1)} %get-tuple-element.41), channel_id=1, source_target_pairs={{0,1},{1,2},{2,3},{3,0},{4,5},{5,6},{6,7},{7,4},{8,9},{9,10},{10,1... | collective-permute-start | bytes 196616 | tf_op jit(solution)/shard_map/ppermute | solution.py:16
  26.7 5.2 %collective-permute-start.6 = (f32[1,128,128]{2,1,0:T(8,128)S(1)}, f32[1,128,128]{2,1,0:T(8,128)S(1)}, u32[]{:S(2)}, u32[]{:S(2)}) collective-permute-start(f32[1,128,128]{2,1,0:T(8,128)S(1)} %slice.270), channel_id=1, source_target_pairs={{0,8},{8,16},{16,24},{24,0},{1,9},{9,17},{17,25},{25,1},{2,10},{10... | collective-permute-start | bytes 196616 | tf_op jit(solution)/shard_map/ppermute | solution.py:16
  31.9 4.3 %collective-permute-start.7 = (f32[1,128,128]{2,1,0:T(8,128)S(1)}, f32[1,128,128]{2,1,0:T(8,128)S(1)}, u32[]{:S(2)}, u32[]{:S(2)}) collective-permute-start(f32[1,128,128]{2,1,0:T(8,128)S(1)} %get-tuple-element.35), channel_id=1, source_target_pairs={{8,0},{16,8},{24,16},{0,24},{9,1},{17,9},{25,17},{1,25},{10,2},{18... | collective-permute-start | bytes 196616 | tf_op jit(solution)/shard_map/ppermute | solution.py:17
  32.6 6.1 %collective-permute-start.11 = (f32[1,128,128]{2,1,0:T(8,128)S(1)}, f32[1,128,128]{2,1,0:T(8,128)S(1)}, u32[]{:S(2)}, u32[]{:S(2)}) collective-permute-start(f32[1,128,128]{2,1,0:T(8,128)S(1)} %get-tuple-element.30), channel_id=1, source_target_pairs={{1,0},{2,1},{3,2},{0,3},{5,4},{6,5},{7,6},{4,7},{9,8},{10,9},{11,1... | collective-permute-start | bytes 196616 | tf_op jit(solution)/shard_map/ppermute | solution.py:17
  32.6 6.1 %collective-permute-start.10 = (f32[1,128,128]{2,1,0:T(8,128)S(1)}, f32[1,128,128]{2,1,0:T(8,128)S(1)}, u32[]{:S(2)}, u32[]{:S(2)}) collective-permute-start(f32[1,128,128]{2,1,0:T(8,128)S(1)} %get-tuple-element.32), channel_id=1, source_target_pairs={{0,1},{1,2},{2,3},{3,0},{4,5},{5,6},{6,7},{7,4},{8,9},{9,10},{10,1... | collective-permute-start | bytes 196616 | tf_op jit(solution)/shard_map/ppermute | solution.py:16
  34.6 1.6 collective-permute-start.8
  34.6 1.6 collective-permute-start.9
  38.7 2.1 %copy-start.2 = (f32[6,128,128]{2,1,0:T(8,128)}, f32[6,128,128]{2,1,0:T(8,128)S(1)}, u32[]{:S(2)}) copy-start(f32[6,128,128]{2,1,0:T(8,128)S(1)} %add_dynamic-update-slice_fusion.18) | copy-start | bytes 1179652
  38.7 2.1 %copy-start.1 = (bf16[1,1,1,768,768]{4,3,2,1,0:T(8,128)(2,1)S(1)}, bf16[1,1,1,768,768]{4,3,2,1,0:T(8,128)(2,1)}, u32[]{:S(2)}) copy-start(bf16[1,1,1,768,768]{4,3,2,1,0:T(8,128)(2,1)} %param.5) | copy-start | bytes 3538948
  44.8 13.7 %copy-start.3 = (f32[6,128,128]{2,1,0:T(8,128)S(1)}, f32[6,128,128]{2,1,0:T(8,128)}, u32[]{:S(2)}) copy-start(f32[6,128,128]{2,1,0:T(8,128)} %copy-done.2) | copy-start | bytes 1179652
  45.0 5.3 %collective-permute-start.12 = (f32[1,128,128]{2,1,0:T(8,128)S(1)}, f32[1,128,128]{2,1,0:T(8,128)S(1)}, u32[]{:S(2)}, u32[]{:S(2)}) collective-permute-start(f32[1,128,128]{2,1,0:T(8,128)S(1)} %slice.276), channel_id=1, source_target_pairs={{0,8},{8,16},{16,24},{24,0},{1,9},{9,17},{17,25},{25,1},{2,10},{10... | collective-permute-start | bytes 196616 | tf_op jit(solution)/shard_map/ppermute | solution.py:16
  50.4 4.6 %collective-permute-start.13 = (f32[1,128,128]{2,1,0:T(8,128)S(1)}, f32[1,128,128]{2,1,0:T(8,128)S(1)}, u32[]{:S(2)}, u32[]{:S(2)}) collective-permute-start(f32[1,128,128]{2,1,0:T(8,128)S(1)} %get-tuple-element.29), channel_id=1, source_target_pairs={{8,0},{16,8},{24,16},{0,24},{9,1},{17,9},{25,17},{1,25},{10,2},{18... | collective-permute-start | bytes 196616 | tf_op jit(solution)/shard_map/ppermute | solution.py:17
  52.4 6.1 %collective-permute-start.17 = (f32[1,128,128]{2,1,0:T(8,128)S(1)}, f32[1,128,128]{2,1,0:T(8,128)S(1)}, u32[]{:S(2)}, u32[]{:S(2)}) collective-permute-start(f32[1,128,128]{2,1,0:T(8,128)S(1)} %get-tuple-element.24), channel_id=1, source_target_pairs={{1,0},{2,1},{3,2},{0,3},{5,4},{6,5},{7,6},{4,7},{9,8},{10,9},{11,1... | collective-permute-start | bytes 196616 | tf_op jit(solution)/shard_map/ppermute | solution.py:17
  52.4 6.1 %collective-permute-start.16 = (f32[1,128,128]{2,1,0:T(8,128)S(1)}, f32[1,128,128]{2,1,0:T(8,128)S(1)}, u32[]{:S(2)}, u32[]{:S(2)}) collective-permute-start(f32[1,128,128]{2,1,0:T(8,128)S(1)} %get-tuple-element.26), channel_id=1, source_target_pairs={{0,1},{1,2},{2,3},{3,0},{4,5},{5,6},{6,7},{7,4},{8,9},{9,10},{10,1... | collective-permute-start | bytes 196616 | tf_op jit(solution)/shard_map/ppermute | solution.py:16
  54.4 1.3 collective-permute-start.14
  54.4 1.4 collective-permute-start.15
  96.5 0.6 copy-start.10
  96.6 0.6 copy-start.12
  97.2 0.5 copy-start.8
  105.6 5.2 %collective-permute-start.18 = (f32[1,128,128]{2,1,0:T(8,128)S(1)}, f32[1,128,128]{2,1,0:T(8,128)S(1)}, u32[]{:S(2)}, u32[]{:S(2)}) collective-permute-start(f32[1,128,128]{2,1,0:T(8,128)S(1)} %slice.282), channel_id=1, source_target_pairs={{0,8},{8,16},{16,24},{24,0},{1,9},{9,17},{17,25},{25,1},{2,10},{10... | collective-permute-start | bytes 196616 | tf_op jit(solution)/shard_map/ppermute | solution.py:16
  110.9 4.3 %collective-permute-start.19 = (f32[1,128,128]{2,1,0:T(8,128)S(1)}, f32[1,128,128]{2,1,0:T(8,128)S(1)}, u32[]{:S(2)}, u32[]{:S(2)}) collective-permute-start(f32[1,128,128]{2,1,0:T(8,128)S(1)} %get-tuple-element.23), channel_id=1, source_target_pairs={{8,0},{16,8},{24,16},{0,24},{9,1},{17,9},{25,17},{1,25},{10,2},{18... | collective-permute-start | bytes 196616 | tf_op jit(solution)/shard_map/ppermute | solution.py:17
  111.9 7.6 %collective-permute-start.23 = (f32[1,128,128]{2,1,0:T(8,128)S(1)}, f32[1,128,128]{2,1,0:T(8,128)S(1)}, u32[]{:S(2)}, u32[]{:S(2)}) collective-permute-start(f32[1,128,128]{2,1,0:T(8,128)S(1)} %get-tuple-element.18), channel_id=1, source_target_pairs={{1,0},{2,1},{3,2},{0,3},{5,4},{6,5},{7,6},{4,7},{9,8},{10,9},{11,1... | collective-permute-start | bytes 196616 | tf_op jit(solution)/shard_map/ppermute | solution.py:17
  113.5 6.1 %collective-permute-start.22 = (f32[1,128,128]{2,1,0:T(8,128)S(1)}, f32[1,128,128]{2,1,0:T(8,128)S(1)}, u32[]{:S(2)}, u32[]{:S(2)}) collective-permute-start(f32[1,128,128]{2,1,0:T(8,128)S(1)} %get-tuple-element.20), channel_id=1, source_target_pairs={{0,1},{1,2},{2,3},{3,0},{4,5},{5,6},{6,7},{7,4},{8,9},{9,10},{10,1... | collective-permute-start | bytes 196616 | tf_op jit(solution)/shard_map/ppermute | solution.py:16
  113.9 1.3 collective-permute-start.20
  113.9 1.4 collective-permute-start.21
  119.6 0.8 copy-start.5
  126.2 7.7 %copy-start.9 = (f32[128]{0:T(128)S(1)}, f32[128]{0:T(128)}, u32[]{:S(2)}) copy-start(f32[128]{0:T(128)} %copy-done.8) | copy-start | bytes 1540
  126.4 5.7 %collective-permute-start.24 = (f32[1,128,128]{2,1,0:T(8,128)S(1)}, f32[1,128,128]{2,1,0:T(8,128)S(1)}, u32[]{:S(2)}, u32[]{:S(2)}) collective-permute-start(f32[1,128,128]{2,1,0:T(8,128)S(1)} %slice.288), channel_id=1, source_target_pairs={{0,8},{8,16},{16,24},{24,0},{1,9},{9,17},{17,25},{25,1},{2,10},{10... | collective-permute-start | bytes 196616 | tf_op jit(solution)/shard_map/ppermute | solution.py:16
  132.2 8.9 %copy-start.6 = (f32[6,128,128]{2,1,0:T(8,128)S(1)}, f32[6,128,128]{2,1,0:T(8,128)}, u32[]{:S(2)}) copy-start(f32[6,128,128]{2,1,0:T(8,128)} %copy-done.5) | copy-start | bytes 1179652
  132.2 46.0 %copy-start.11 = (f32[128]{0:T(128)S(1)}, f32[128]{0:T(128)}, u32[]{:S(2)}) copy-start(f32[128]{0:T(128)} %copy-done.10) | copy-start | bytes 1540
  132.2 46.0 %copy-start.13 = (f32[128]{0:T(128)S(1)}, f32[128]{0:T(128)}, u32[]{:S(2)}) copy-start(f32[128]{0:T(128)} %copy-done.12) | copy-start | bytes 1540
  132.2 46.0 %copy-start.4 = (f32[6,128,128]{2,1,0:T(8,128)S(1)}, f32[6,128,128]{2,1,0:T(8,128)}, u32[]{:S(2)}) copy-start(f32[6,128,128]{2,1,0:T(8,128)} %copy-done.2) | copy-start | bytes 1179652
  132.2 4.4 %collective-permute-start.25 = (f32[1,128,128]{2,1,0:T(8,128)S(1)}, f32[1,128,128]{2,1,0:T(8,128)S(1)}, u32[]{:S(2)}, u32[]{:S(2)}) collective-permute-start(f32[1,128,128]{2,1,0:T(8,128)S(1)} %get-tuple-element.17), channel_id=1, source_target_pairs={{8,0},{16,8},{24,16},{0,24},{9,1},{17,9},{25,17},{1,25},{10,2},{18... | collective-permute-start | bytes 196616 | tf_op jit(solution)/shard_map/ppermute | solution.py:17
  134.0 7.1 %collective-permute-start.29 = (f32[1,128,128]{2,1,0:T(8,128)S(1)}, f32[1,128,128]{2,1,0:T(8,128)S(1)}, u32[]{:S(2)}, u32[]{:S(2)}) collective-permute-start(f32[1,128,128]{2,1,0:T(8,128)S(1)} %get-tuple-element.12), channel_id=1, source_target_pairs={{1,0},{2,1},{3,2},{0,3},{5,4},{6,5},{7,6},{4,7},{9,8},{10,9},{11,1... | collective-permute-start | bytes 196616 | tf_op jit(solution)/shard_map/ppermute | solution.py:17
  135.0 6.1 %collective-permute-start.28 = (f32[1,128,128]{2,1,0:T(8,128)S(1)}, f32[1,128,128]{2,1,0:T(8,128)S(1)}, u32[]{:S(2)}, u32[]{:S(2)}) collective-permute-start(f32[1,128,128]{2,1,0:T(8,128)S(1)} %get-tuple-element.14), channel_id=1, source_target_pairs={{0,1},{1,2},{2,3},{3,0},{4,5},{5,6},{6,7},{7,4},{8,9},{9,10},{10,1... | collective-permute-start | bytes 196616 | tf_op jit(solution)/shard_map/ppermute | solution.py:16
  136.1 1.3 collective-permute-start.26
  136.1 1.4 collective-permute-start.27
where the time goes:
time: 180 us; the launch traced here: 179 us
  blocking collectives  75 us (42%)
  waiting for transfers between devices  36.6 us (20%)
  starting transfers between devices  29.8 us (17%)
  local copies, waits for them, and re-layouts  25.1 us (14%)
  other arithmetic  6.8 us (4%)
  matrix products  4.57 us (3%)
    psum x2, blocking collectives, inner_pair(): return lax.psum((gamma_part, delta_part), ('gx', 'gy', 'gz'))  75 us
    ppermute x15, waiting for transfers between devices, with_halo(): before = lax.ppermute(last, axis, up)  34.4 us
    ppermute x15, starting transfers between devices, with_halo(): after = lax.ppermute(first, axis, down)  17.1 us
    ppermute x15, starting transfers between devices, with_halo(): before = lax.ppermute(last, axis, up)  12.7 us
    gather x4, local copies, waits for them, and re-layouts, local_product(): restricted = signed[inverse].astype(jnp.bfloat16)  8.17 us
    gather x4, local copies, waits for them, and re-layouts, local_product(): return signs * product[face_rows].reshape(6, width, columns)  7.01 us
    dot_general x4, matrix products, local_product(): product = jnp.dot(operator, restricted, preferred_element_type=jnp.float32)  4.57 us
  transfers between devices with their start and end apart: 30, of which 16 were waited for; matrix products, arithmetic and copies ran while one was open for 4% of the time, Pallas kernels for 0%

commit v1 on v0

v1 whole, which is shorter than its diff:
```python
import functools
import jax
import jax.numpy as jnp
from jax import lax
from jax.experimental import pallas as pl
from jax.experimental.pallas import tpu as pltpu
from jax.sharding import PartitionSpec as P

AXES = ("gx", "gy", "gz")
ARRIVAL = (1, 0, 2)
MESH = pl.DeviceIdType.MESH


def kernel(
    sizes, stiff_hbm, flex_hbm, load_hbm, map_ref, sign_ref, mult_ref, res_ref,
    raw, mid, ops, load, own, got, acc, vec, gat_x, gat_y, gat_z,
    local_sem, send_sem, recv_sem, sx, rx, sy, ry, sz, rz,
):
    width, columns = load.shape[1:]
    pair = 2 * width
    me = [lax.axis_index(axis) for axis in AXES]

    local = [
        pltpu.make_async_copy(load_hbm, load, local_sem.at[0]),
        pltpu.make_async_copy(stiff_hbm, raw.at[0], local_sem.at[1]),
        pltpu.make_async_copy(flex_hbm, raw.at[1], local_sem.at[2]),
    ]
    for copy in local:
        copy.start()

    barrier = pltpu.get_barrier_semaphore()
    for d, axis in enumerate(AXES):
        for k in range(1, sizes[d]):
            pl.semaphore_signal(
                barrier, inc=1, device_id={axis: lax.rem(me[d] + k, sizes[d])}, device_id_type=MESH
            )
    pl.semaphore_wait(barrier, sum(sizes) - 3)

    sent = []

    def send_face(exchange, face, source):
        d, upper = face // 2, face % 2
        step = 1 if upper else sizes[d] - 1
        there = face - 1 if upper else face + 1
        copy = pltpu.make_async_remote_copy(
            src_ref=source.at[face],
            dst_ref=got.at[exchange, there],
            send_sem=send_sem.at[exchange, face],
            recv_sem=recv_sem.at[exchange, there],
            device_id={AXES[d]: lax.rem(me[d] + step, sizes[d])},
            device_id_type=MESH,
        )
        copy.start()
        sent.append(copy)
        return copy

    gathers = ((gat_x, sx, rx), (gat_y, sy, ry), (gat_z, sz, rz))

    def gather_start(which, d, value):
        buf, ssem, rsem = gathers[d]
        buf[which, me[d]] = value
        for k in range(1, sizes[d]):
            peer = lax.rem(me[d] + k, sizes[d])
            copy = pltpu.make_async_remote_copy(
                src_ref=buf.at[which, me[d]],
                dst_ref=buf.at[which, me[d]],
                send_sem=ssem.at[which, k],
                recv_sem=rsem.at[which, me[d]],
                device_id={AXES[d]: peer},
                device_id_type=MESH,
            )
            copy.start()
            sent.append(copy)

    def gather_finish(which, d):
        buf, ssem, rsem = gathers[d]
        for k in range(1, sizes[d]):
            peer = lax.rem(me[d] + k, sizes[d])
            pltpu.make_async_remote_copy(
                src_ref=buf.at[which, peer],
                dst_ref=buf.at[which, peer],
                send_sem=ssem.at[which, k],
                recv_sem=rsem.at[which, peer],
                device_id={AXES[d]: peer},
                device_id_type=MESH,
            ).wait_recv()
        total = buf[which, 0]
        for k in range(1, sizes[d]):
            total = total + buf[which, k]
        return total

    def rows(d):
        return slice(d * pair, (d + 1) * pair)

    def flat(value):
        return value.reshape(pair, columns)

    def faces(ref, d):
        return flat(ref[2 * d : 2 * d + 2])

    def fold(which):
        for d in range(3):
            low = map_ref[2 * d : 2 * d + 1, :]
            high = map_ref[2 * d + 1 : 2 * d + 2, :] + width
            row = jnp.concatenate([low, high], axis=1)
            sign = jnp.concatenate(
                [sign_ref[2 * d : 2 * d + 1, :], sign_ref[2 * d + 1 : 2 * d + 2, :]], axis=1
            ).astype(jnp.float32)
            place = lax.broadcasted_iota(jnp.int32, (pair, pair), 0)
            pick = jnp.where(place == row, sign, 0.0)
            mid[:, rows(d)] = jnp.dot(
                raw[which, :, rows(d)], pick.astype(jnp.bfloat16), preferred_element_type=jnp.float32
            ).astype(jnp.bfloat16)
        for d in range(3):
            low = map_ref[2 * d : 2 * d + 1, :]
            high = map_ref[2 * d + 1 : 2 * d + 2, :] + width
            row = jnp.concatenate([low, high], axis=1)
            sign = jnp.concatenate(
                [sign_ref[2 * d : 2 * d + 1, :], sign_ref[2 * d + 1 : 2 * d + 2, :]], axis=1
            ).astype(jnp.float32)
            place = lax.broadcasted_iota(jnp.int32, (pair, pair), 0)
            pick = jnp.where(place == row, sign, 0.0).T
            ops[which, rows(d), :] = jnp.dot(
                pick.astype(jnp.bfloat16), mid[rows(d), :], preferred_element_type=jnp.float32
            ).astype(jnp.bfloat16)

    def product(block, value, split):
        high = value.astype(jnp.bfloat16)
        if not split:
            return jnp.dot(block, high, preferred_element_type=jnp.float32)
        low = (value - high.astype(jnp.float32)).astype(jnp.bfloat16)
        both = jnp.dot(block, jnp.concatenate([high, low], axis=1), preferred_element_type=jnp.float32)
        return both[:, :columns] + both[:, columns:]

    def apply(which, get, out, split, ready=None):
        first = product(ops[which, :, rows(ARRIVAL[0])], get(ARRIVAL[0]), split)
        acc[...] = first
        acc[...] += product(ops[which, :, rows(ARRIVAL[1])], get(ARRIVAL[1]), split)
        last = get(ARRIVAL[2])
        for d in reversed(ARRIVAL):
            value = acc[rows(d), :] + product(ops[which, rows(d), rows(ARRIVAL[2])], last, split)
            own[out, 2 * d : 2 * d + 2] = value.reshape(2, width, columns)
            if ready is not None:
                ready(d)

    def sender(exchange):
        def ready(d):
            waits[exchange, 2 * d + 1] = send_face(exchange, 2 * d, own.at[exchange - 1])
            waits[exchange, 2 * d] = send_face(exchange, 2 * d + 1, own.at[exchange - 1])

        return ready

    waits = {}

    def arrive(exchange, d):
        waits[exchange, 2 * d].wait_recv()
        waits[exchange, 2 * d + 1].wait_recv()
        return flat(got[exchange, 2 * d : 2 * d + 2])

    def inner(first, second):
        total = jnp.zeros((8, columns), jnp.float32)
        for d in range(3):
            term = faces(first, d) * faces(second, d)
            total = total + jnp.sum(term.reshape(pair // 8, 8, columns), axis=0)
        return total

    def down(value):
        return jnp.sum(value, axis=0, keepdims=True)

    r0, z0, w0, r1, z1 = (vec.at[k] for k in range(5))

    def keep(ref, d, value):
        ref[2 * d : 2 * d + 2] = value.reshape(2, width, columns)
        return value

    for d in reversed(ARRIVAL):
        waits[0, 2 * d + 1] = send_face(0, 2 * d, load_hbm)
        waits[0, 2 * d] = send_face(0, 2 * d + 1, load_hbm)
    local[1].wait()
    fold(0)
    local[0].wait()
    apply(0, lambda d: keep(r0, d, faces(load, d) + arrive(0, d)), 0, True, sender(1))
    gamma_part = inner(r0, own.at[0])
    local[2].wait()
    fold(1)

    apply(1, lambda d: keep(z0, d, faces(own.at[0], d) + arrive(1, d)), 1, False)
    gather_start(0, 1, jnp.stack([gamma_part, inner(z0, own.at[1])]))
    for d in reversed(ARRIVAL):
        sender(2)(d)
    gather_start(0, 0, gather_finish(0, 1))

    apply(0, lambda d: keep(w0, d, faces(own.at[1], d) + arrive(2, d)), 2, True, sender(3))
    gather_start(0, 2, gather_finish(0, 0))
    sums = gather_finish(0, 2)
    gamma0, delta0 = down(sums[0]), down(sums[1])
    alpha0 = gamma0 / delta0

    gamma_part = jnp.zeros((8, columns), jnp.float32)
    for d in range(3):
        value = keep(r1, d, faces(r0, d) - alpha0 * faces(w0, d))
        term = value * (faces(own.at[0], d) - alpha0 * faces(own.at[2], d))
        gamma_part = gamma_part + jnp.sum(term.reshape(pair // 8, 8, columns), axis=0)

    apply(
        1,
        lambda d: keep(z1, d, faces(z0, d) - alpha0 * (faces(own.at[2], d) + arrive(3, d))),
        3,
        False,
    )
    gather_start(1, 1, jnp.stack([gamma_part, inner(z1, own.at[3])]))
    for d in reversed(ARRIVAL):
        waits[4, 2 * d] = send_face(4, 2 * d + 1, own.at[3])
    gather_start(1, 0, gather_finish(1, 1))
    gather_start(1, 2, gather_finish(1, 0))
    sums = gather_finish(1, 2)
    gamma1, delta1 = down(sums[0]), down(sums[1])
    beta = gamma1 / gamma0
    alpha1 = gamma1 / (delta1 - beta * gamma1 / alpha0)
    for d in ARRIVAL:
        mult_ref[d] = alpha0 * z0[2 * d] + alpha1 * (z1[2 * d] + beta * z0[2 * d])
    for d in ARRIVAL:
        waits[4, 2 * d].wait_recv()
        image = own[3, 2 * d] + got[4, 2 * d] + beta * w0[2 * d]
        res_ref[d] = r1[2 * d] - alpha1 * image
    for copy in sent:
        copy.wait_send()


def shards(sizes, flexibility, stiffness, local_load, face_map, face_sign):
    order = flexibility.shape[-1]
    _, width, columns = local_load.shape[-3:]
    whole = (6, width, columns)
    half = (3, width, columns)
    dma = pltpu.SemaphoreType.DMA
    scratch = [
        pltpu.VMEM((2, order, order), jnp.bfloat16),
        pltpu.VMEM((order, order), jnp.bfloat16),
        pltpu.VMEM((2, order, order), jnp.bfloat16),
        pltpu.VMEM(whole, jnp.float32),
        pltpu.VMEM((4,) + whole, jnp.float32),
        pltpu.VMEM((5,) + whole, jnp.float32),
        pltpu.VMEM((order, columns), jnp.float32),
        pltpu.VMEM((5,) + whole, jnp.float32),
    ]
    scratch += [pltpu.VMEM((2, n, 2, 8, columns), jnp.float32) for n in sizes]
    scratch += [dma((3,)), dma((5, 6)), dma((5, 6))]
    for n in sizes:
        scratch += [dma((2, n)), dma((2, n))]
    any_space = pl.BlockSpec(memory_space=pl.ANY)
    vmem = pl.BlockSpec(memory_space=pltpu.VMEM)
    multipliers, residual = pl.pallas_call(
        functools.partial(kernel, sizes),
        out_shape=[jax.ShapeDtypeStruct(half, jnp.float32)] * 2,
        in_specs=[any_space, any_space, any_space, vmem, vmem],
        out_specs=[vmem, vmem],
        scratch_shapes=scratch,
        compiler_params=pltpu.CompilerParams(
            collective_id=0, has_side_effects=True, vmem_limit_bytes=60 * 1024 * 1024
        ),
        cost_estimate=pl.CostEstimate(
            flops=16 * order * order * columns, bytes_accessed=4 * order * order, transcendentals=0
        ),
    )(
        stiffness.reshape(order, order),
        flexibility.reshape(order, order),
        local_load.reshape(whole),
        face_map.reshape(6, width),
        face_sign.reshape(6, width),
    )
    return multipliers[None, None, None], residual[None, None, None]


def solution(mesh):
    sizes = tuple(mesh.shape[axis] for axis in AXES)
    matrix, face, line = (P(*AXES, *([None] * k)) for k in (2, 3, 2))
    return jax.shard_map(
        functools.partial(shards, sizes),
        mesh=mesh,
        in_specs=(matrix, matrix, face, line, line),
        out_specs=(face, face),
        check_vma=False,
    )
```

time: 180 us -> 42.4 us (0.24)
  blocking collectives: 75 us -> 0 us
  Pallas kernels: 0 us -> 37 us
  waiting for transfers between devices: 36.6 us -> 0 us
  starting transfers between devices: 29.8 us -> 0 us
  local copies, waits for them, and re-layouts: 25.1 us -> 4.53 us
  other arithmetic: 6.8 us -> 0 us
  matrix products: 4.57 us -> 0 us
    psum x2 -> x0, blocking collectives: 75 us -> none  [inner_pair(): return lax.psum((gamma_part, delta_part), ('gx', 'gy', 'gz'))]
    pallas_call x0 -> x1, Pallas kernels: none -> 37 us  [shards(): pl.pallas_call(functools.partial(kernel, sizes), out_shape=[jax.ShapeDtyp...]
    ppermute x30 -> x0, waiting for transfers between devices: 36.6 us -> none  [the longest x15 34.4 us: with_halo(): before = lax.ppermute(last, axis, up)]
    ppermute x30 -> x0, starting transfers between devices: 29.8 us -> none  [the longest x15 17.1 us: with_halo(): after = lax.ppermute(first, axis, down)]
    gather x8 -> x0, local copies, waits for them, and re-layouts: 15.2 us -> none  [the longest x4 8.17 us: local_product(): restricted = signed[inverse].astype(jnp.bfloat16)]
    dot_general x4 -> x0, matrix products: 4.57 us -> none  [local_product(): product = jnp.dot(operator, restricted, preferred_element_type=jnp.float32)]
    scatter x1 -> x0, local copies, waits for them, and re-layouts: 3.38 us -> none  [shards(): jnp.zeros((6 * width,), jnp.int32).at[face_rows]]
    dot_general x4 -> x0, local copies, waits for them, and re-layouts: 2.61 us -> none  [local_product(): product = jnp.dot(operator, restricted, preferred_element_type=jnp.float32)]
  transfers between devices with their start and end apart: 30 -> 0, of which waited for: 16 -> 0; matrix products, arithmetic and copies ran while one was open for 4% -> 0% of each run, Pallas kernels for 0% -> 0%
where the time goes in v1:
time: 42.4 us; the launch traced here: 42.2 us
  Pallas kernels  37 us (87%)
  local copies, waits for them, and re-layouts  4.53 us (11%)
  between operations  0.64 us (2%)
    pallas_call x1, Pallas kernels, shards(): pl.pallas_call(functools.partial(kernel, sizes), out_shape=[jax.ShapeDtyp...  37 us
    unnamed x3, local copies, waits for them, and re-layouts  4.53 us

profile of v1, /device:TPU:0, one launch (start us, length us, event | category | flops | bytes accessed | tf_op | source)
XLA Modules:
  0.0 42.2 jit_solution(429338651489050858)
XLA Ops:
  0.6 1.3 %copy_bitcast_fusion = (s32[6,128]{1,0:T(8,128)}, s32[6,128]{1,0:T(8,128)}) fusion(s32[1,1,1,6,128]{4,2,3,1,0:T(1,128)} %param.9, s32[1,1,1,6,128]{4,2,3,1,0:T(1,128)} %param.8), kind=kLoop, calls=%fused_computation | loop fusion | bytes 12288
  1.9 37.0 %shard_map.68 = (f32[3,128,128]{2,1,0:T(8,128)}, f32[3,128,128]{2,1,0:T(8,128)}) custom-call(bf16[768,768]{1,0:T(8,128)(2,1)} %bitcast.11, bf16[768,768]{1,0:T(8,128)(2,1)} %bitcast.12, f32[6,128,128]{2,1,0:T(8,128)} %bitcast.13, s32[6,128]{1,0:T(8,128)} %get-tuple-element.7.map_ref, s32[6,128]{1,0:T(8,128)} %get-tuple-element.6.sign_ref), custom_call_target="tpu_custom_call" | custom-call | flops 1207959552 | bytes 2359296 | tf_op jit(solution)/shard_map/pallas_call | solution.py:252
  38.9 1.6 %copy.13 = f32[1,1,1,3,128,128]{5,4,3,2,1,0:T(8,128)} copy(f32[1,1,1,3,128,128]{5,4,3,2,1,0:T(8,128)} %bitcast.10) | data formatting | bytes 393216
  40.5 1.6 %copy.14 = f32[1,1,1,3,128,128]{5,4,3,2,1,0:T(8,128)} copy(f32[1,1,1,3,128,128]{5,4,3,2,1,0:T(8,128)} %bitcast.9) | data formatting | bytes 393216

commit v2 on v1

--- a/solution.py
+++ b/solution.py
@@ -1,4 +1,6 @@
 import functools
+import itertools
+import math
 import jax
 import jax.numpy as jnp
 from jax import lax
@@ -11,10 +13,22 @@
 MESH = pl.DeviceIdType.MESH
 
 
+def peers(sizes, me, group):
+    found = []
+    for offsets in itertools.product(*[range(sizes[d]) for d in group]):
+        if any(offsets):
+            where, slot = {}, 0
+            for d, k in zip(group, offsets):
+                index = lax.rem(me[d] + k, sizes[d]) if k else me[d]
+                where[AXES[d]] = index
+                slot = slot * sizes[d] + index
+            found.append((where, slot))
+    return found
+
+
 def kernel(
-    sizes, stiff_hbm, flex_hbm, load_hbm, map_ref, sign_ref, mult_ref, res_ref,
-    raw, mid, ops, load, own, got, acc, vec, gat_x, gat_y, gat_z,
-    local_sem, send_sem, recv_sem, sx, rx, sy, ry, sz, rz,
+    sizes, groups, stiff_hbm, flex_hbm, load_hbm, map_ref, sign_ref, mult_ref, res_ref,
+    raw, mid, ops, load, own, got, acc, vec, local_sem, send_sem, recv_sem, *gathers
 ):
     width, columns = load.shape[1:]
     pair = 2 * width
@@ -29,12 +43,10 @@
         copy.start()
 
     barrier = pltpu.get_barrier_semaphore()
-    for d, axis in enumerate(AXES):
-        for k in range(1, sizes[d]):
-            pl.semaphore_signal(
-                barrier, inc=1, device_id={axis: lax.rem(me[d] + k, sizes[d])}, device_id_type=MESH
-            )
-    pl.semaphore_wait(barrier, sum(sizes) - 3)
+    others = [peer for group in groups for peer in peers(sizes, me, group)]
+    for where, _ in others:
+        pl.semaphore_signal(barrier, inc=1, device_id=where, device_id_type=MESH)
+    pl.semaphore_wait(barrier, len(others))
 
     sent = []
 
@@ -54,40 +66,40 @@
         sent.append(copy)
         return copy
 
-    gathers = ((gat_x, sx, rx), (gat_y, sy, ry), (gat_z, sz, rz))
-
-    def gather_start(which, d, value):
-        buf, ssem, rsem = gathers[d]
-        buf[which, me[d]] = value
-        for k in range(1, sizes[d]):
-            peer = lax.rem(me[d] + k, sizes[d])
+    def slot_of(group):
+        index = 0
+        for d in group:
+            index = index * sizes[d] + me[d]
+        return index
+
+    def gather_start(which, stage, value):
+        buf, ssem, rsem = gathers[3 * stage : 3 * stage + 3]
+        mine = slot_of(groups[stage])
+        buf[which, mine] = value
+        for k, (where, _) in enumerate(peers(sizes, me, groups[stage])):
             copy = pltpu.make_async_remote_copy(
-                src_ref=buf.at[which, me[d]],
-                dst_ref=buf.at[which, me[d]],
+                src_ref=buf.at[which, mine],
+                dst_ref=buf.at[which, mine],
                 send_sem=ssem.at[which, k],
-                recv_sem=rsem.at[which, me[d]],
-                device_id={AXES[d]: peer},
+                recv_sem=rsem.at[which, mine],
+                device_id=where,
                 device_id_type=MESH,
             )
             copy.start()
             sent.append(copy)
 
-    def gather_finish(which, d):
-        buf, ssem, rsem = gathers[d]
-        for k in range(1, sizes[d]):
-            peer = lax.rem(me[d] + k, sizes[d])
+    def gather_finish(which, stage):
+        buf, ssem, rsem = gathers[3 * stage : 3 * stage + 3]
+        for k, (where, slot) in enumerate(peers(sizes, me, groups[stage])):
             pltpu.make_async_remote_copy(
-                src_ref=buf.at[which, peer],
-                dst_ref=buf.at[which, peer],
+                src_ref=buf.at[which, slot],
+                dst_ref=buf.at[which, slot],
                 send_sem=ssem.at[which, k],
-                recv_sem=rsem.at[which, peer],
-                device_id={AXES[d]: peer},
+                recv_sem=rsem.at[which, slot],
+                device_id=where,
                 device_id_type=MESH,
             ).wait_recv()
-        total = buf[which, 0]
-        for k in range(1, sizes[d]):
-            total = total + buf[which, k]
-        return total
+        return jnp.sum(buf[which], axis=0)
 
     def rows(d):
         return slice(d * pair, (d + 1) * pair)
@@ -100,11 +112,11 @@
 
     def fold(which):
         for d in range(3):
-            low = map_ref[2 * d : 2 * d + 1, :]
-            high = map_ref[2 * d + 1 : 2 * d + 2, :] + width
+            low = map_ref[2 * d]
+            high = map_ref[2 * d + 1] + width
             row = jnp.concatenate([low, high], axis=1)
             sign = jnp.concatenate(
-                [sign_ref[2 * d : 2 * d + 1, :], sign_ref[2 * d + 1 : 2 * d + 2, :]], axis=1
+                [sign_ref[2 * d], sign_ref[2 * d + 1]], axis=1
             ).astype(jnp.float32)
             place = lax.broadcasted_iota(jnp.int32, (pair, pair), 0)
             pick = jnp.where(place == row, sign, 0.0)
@@ -112,11 +124,11 @@
                 raw[which, :, rows(d)], pick.astype(jnp.bfloat16), preferred_element_type=jnp.float32
             ).astype(jnp.bfloat16)
         for d in range(3):
-            low = map_ref[2 * d : 2 * d + 1, :]
-            high = map_ref[2 * d + 1 : 2 * d + 2, :] + width
+            low = map_ref[2 * d]
+            high = map_ref[2 * d + 1] + width
             row = jnp.concatenate([low, high], axis=1)
             sign = jnp.concatenate(
-                [sign_ref[2 * d : 2 * d + 1, :], sign_ref[2 * d + 1 : 2 * d + 2, :]], axis=1
+                [sign_ref[2 * d], sign_ref[2 * d + 1]], axis=1
             ).astype(jnp.float32)
             place = lax.broadcasted_iota(jnp.int32, (pair, pair), 0)
             pick = jnp.where(place == row, sign, 0.0).T
@@ -164,8 +176,10 @@
             total = total + jnp.sum(term.reshape(pair // 8, 8, columns), axis=0)
         return total
 
-    def down(value):
-        return jnp.sum(value, axis=0, keepdims=True)
+    def both(first, second):
+        return jnp.concatenate(
+            [jnp.sum(value, axis=0, keepdims=True) for value in (first, second)], axis=0
+        )
 
     r0, z0, w0, r1, z1 = (vec.at[k] for k in range(5))
 
@@ -184,16 +198,16 @@
     local[2].wait()
     fold(1)
 
-    apply(1, lambda d: keep(z0, d, faces(own.at[0], d) + arrive(1, d)), 1, False)
-    gather_start(0, 1, jnp.stack([gamma_part, inner(z0, own.at[1])]))
+    apply(1, lambda d: keep(z0, d, faces(own.at[0], d) + arrive(1, d)), 1, True)
+    gather_start(0, 0, both(gamma_part, inner(z0, own.at[1])))
     for d in reversed(ARRIVAL):
         sender(2)(d)
-    gather_start(0, 0, gather_finish(0, 1))
+    for stage in range(1, len(groups)):
+        gather_start(0, stage, gather_finish(0, stage - 1))
 
     apply(0, lambda d: keep(w0, d, faces(own.at[1], d) + arrive(2, d)), 2, True, sender(3))
-    gather_start(0, 2, gather_finish(0, 0))
-    sums = gather_finish(0, 2)
-    gamma0, delta0 = down(sums[0]), down(sums[1])
+    sums = gather_finish(0, len(groups) - 1)
+    gamma0, delta0 = sums[0:1], sums[1:2]
     alpha0 = gamma0 / delta0
 
     gamma_part = jnp.zeros((8, columns), jnp.float32)
@@ -206,15 +220,15 @@
         1,
         lambda d: keep(z1, d, faces(z0, d) - alpha0 * (faces(own.at[2], d) + arrive(3, d))),
         3,
-        False,
+        True,
     )
-    gather_start(1, 1, jnp.stack([gamma_part, inner(z1, own.at[3])]))
+    gather_start(1, 0, both(gamma_part, inner(z1, own.at[3])))
     for d in reversed(ARRIVAL):
         waits[4, 2 * d] = send_face(4, 2 * d + 1, own.at[3])
-    gather_start(1, 0, gather_finish(1, 1))
-    gather_start(1, 2, gather_finish(1, 0))
-    sums = gather_finish(1, 2)
-    gamma1, delta1 = down(sums[0]), down(sums[1])
+    for stage in range(1, len(groups)):
+        gather_start(1, stage, gather_finish(1, stage - 1))
+    sums = gather_finish(1, len(groups) - 1)
+    gamma1, delta1 = sums[0:1], sums[1:2]
     beta = gamma1 / gamma0
     alpha1 = gamma1 / (delta1 - beta * gamma1 / alpha0)
     for d in ARRIVAL:
@@ -225,6 +239,17 @@
         res_ref[d] = r1[2 * d] - alpha1 * image
     for copy in sent:
         copy.wait_send()
+
+
+def hand_over(mult_in, res_in, mult_out, res_out, sem):
+    copies = [
+        pltpu.make_async_copy(mult_in, mult_out, sem.at[0]),
+        pltpu.make_async_copy(res_in, res_out, sem.at[1]),
+    ]
+    for copy in copies:
+        copy.start()
+    for copy in copies:
+        copy.wait()
 
 
 def shards(sizes, flexibility, stiffness, local_load, face_map, face_sign):
@@ -243,16 +268,17 @@
         pltpu.VMEM((order, columns), jnp.float32),
         pltpu.VMEM((5,) + whole, jnp.float32),
     ]
-    scratch += [pltpu.VMEM((2, n, 2, 8, columns), jnp.float32) for n in sizes]
     scratch += [dma((3,)), dma((5, 6)), dma((5, 6))]
-    for n in sizes:
-        scratch += [dma((2, n)), dma((2, n))]
-    any_space = pl.BlockSpec(memory_space=pl.ANY)
+    groups = ((1, 0, 2),) if math.prod(sizes) <= 64 else ((1,), (0,), (2,))
+    for group in groups:
+        n = math.prod(sizes[d] for d in group)
+        scratch += [pltpu.VMEM((2, n, 2, columns), jnp.float32), dma((2, n)), dma((2, n))]
+    hbm = pl.BlockSpec(memory_space=pltpu.HBM)
     vmem = pl.BlockSpec(memory_space=pltpu.VMEM)
     multipliers, residual = pl.pallas_call(
-        functools.partial(kernel, sizes),
+        functools.partial(kernel, sizes, groups),
         out_shape=[jax.ShapeDtypeStruct(half, jnp.float32)] * 2,
-        in_specs=[any_space, any_space, any_space, vmem, vmem],
+        in_specs=[hbm, hbm, hbm, vmem, vmem],
         out_specs=[vmem, vmem],
         scratch_shapes=scratch,
         compiler_params=pltpu.CompilerParams(
@@ -265,9 +291,16 @@
         stiffness.reshape(order, order),
         flexibility.reshape(order, order),
         local_load.reshape(whole),
-        face_map.reshape(6, width),
-        face_sign.reshape(6, width),
+        face_map.reshape(6, 1, width),
+        face_sign.reshape(6, 1, width),
     )
+    multipliers, residual = pl.pallas_call(
+        hand_over,
+        out_shape=[jax.ShapeDtypeStruct(half, jnp.float32)] * 2,
+        in_specs=[vmem, vmem],
+        out_specs=[hbm, hbm],
+        scratch_shapes=[dma((2,))],
+    )(multipliers, residual)
     return multipliers[None, None, None], residual[None, None, None]
 
 

time: 42.4 us -> 38.1 us (0.90)
  local copies, waits for them, and re-layouts: 4.53 us -> 0 us
    unnamed x3 -> x0, local copies, waits for them, and re-layouts: 4.53 us -> none
    pallas_call x1 -> x2, Pallas kernels: 37 us -> 37.2 us  [the longest x1 35.4 us: shards(): pl.pallas_call(functools.partial(kernel, sizes, groups), out_shape=[jax.S...]
where the time goes in v2:
time: 38.1 us; the launch traced here: 37.9 us
  Pallas kernels  37.2 us (98%)
  between operations  0.64 us (2%)
    pallas_call x1, Pallas kernels, shards(): pl.pallas_call(functools.partial(kernel, sizes, groups), out_shape=[jax.S...  35.4 us
    pallas_call x1, Pallas kernels, shards(): pl.pallas_call(hand_over, out_shape=[jax.ShapeDtypeStruct(half, jnp.float...  1.78 us

profile of v2, /device:TPU:0, one launch (start us, length us, event | category | flops | bytes accessed | tf_op | source)
XLA Modules:
  0.0 37.9 jit_solution(4076587175364952488)
XLA Ops:
  0.6 35.4 %shard_map.68 = (f32[3,128,128]{2,1,0:T(8,128)}, f32[3,128,128]{2,1,0:T(8,128)}) custom-call(bf16[768,768]{1,0:T(8,128)(2,1)} %bitcast.7, bf16[768,768]{1,0:T(8,128)(2,1)} %bitcast.8, f32[6,128,128]{2,1,0:T(8,128)} %bitcast.9, s32[6,1,128]{2,1,0:T(1,128)} %bitcast.12, s32[6,1,128]{2,1,0:T(1,128)} %bitcast.13), custom_call_target="tpu_custom_call" | custom-call | flops 1207959552 | bytes 2359296 | tf_op jit(solution)/shard_map/pallas_call | solution.py:278
  36.1 1.8 %shard_map.69 = (f32[3,128,128]{2,1,0:T(8,128)}, f32[3,128,128]{2,1,0:T(8,128)}) custom-call(f32[3,128,128]{2,1,0:T(8,128)} %get-tuple-element.6.mult_in, f32[3,128,128]{2,1,0:T(8,128)} %get-tuple-element.7.res_in), custom_call_target="tpu_custom_call" | custom-call | tf_op jit(solution)/shard_map/pallas_call | solution.py:297

commit v3 on v2

v3 whole, which is shorter than its diff:
```python
import functools
import itertools
import math
import jax
import jax.numpy as jnp
from jax import lax
from jax.experimental import pallas as pl
from jax.experimental.pallas import tpu as pltpu
from jax.sharding import PartitionSpec as P

AXES = ("gx", "gy", "gz")
ARRIVAL = (1, 0, 2)
MESH = pl.DeviceIdType.MESH


def peers(sizes, me, group):
    found = []
    for offsets in itertools.product(*[range(sizes[d]) for d in group]):
        if any(offsets):
            where, slot = {}, 0
            for d, k in zip(group, offsets):
                index = lax.rem(me[d] + k, sizes[d]) if k else me[d]
                where[AXES[d]] = index
                slot = slot * sizes[d] + index
            found.append((where, slot))
    return found


def kernel(
    sizes, groups, stiff_hbm, flex_hbm, load_hbm, map_ref, sign_ref, mult_ref, res_ref,
    raw, mid, ops, load, begin, own, got, acc, vec, local_sem, send_sem, recv_sem, *gathers
):
    width, columns = load.shape[1:]
    pair, short, lanes = 2 * width, width // 2, columns // 2
    me = [lax.axis_index(axis) for axis in AXES]

    local = [
        pltpu.make_async_copy(load_hbm, load, local_sem.at[0]),
        pltpu.make_async_copy(stiff_hbm, raw.at[0], local_sem.at[1]),
        pltpu.make_async_copy(flex_hbm, raw.at[1], local_sem.at[2]),
    ]
    for copy in local:
        copy.start()

    barrier = pltpu.get_barrier_semaphore()
    others = [peer for group in groups for peer in peers(sizes, me, group)]
    for where, _ in others:
        pl.semaphore_signal(barrier, inc=1, device_id=where, device_id_type=MESH)

    def turn(value):
        return pltpu.roll(value, lanes, 1)

    def merge(first, second):
        lane = lax.broadcasted_iota(jnp.int32, first.shape, 1)
        return jnp.where(lane < lanes, first, second)

    local[0].wait()
    for face in range(6):
        top, bottom = load[face, :short], load[face, short:]
        begin[0, face] = merge(top, turn(bottom))
        begin[1, face] = merge(turn(top), bottom)
    pl.semaphore_wait(barrier, len(others))

    sent = []
    waits = {}

    def send_face(half, exchange, face, source):
        d, upper = face // 2, face % 2
        step = 1 if upper else sizes[d] - 1
        there = face - 1 if upper else face + 1
        copy = pltpu.make_async_remote_copy(
            src_ref=source.at[face],
            dst_ref=got.at[half, exchange, there],
            send_sem=send_sem.at[half, exchange, face],
            recv_sem=recv_sem.at[half, exchange, there],
            device_id={AXES[d]: lax.rem(me[d] + step, sizes[d])},
            device_id_type=MESH,
        )
        copy.start()
        sent.append(copy)
        waits[half, exchange, there] = copy

    def slot_of(group):
        index = 0
        for d in group:
            index = index * sizes[d] + me[d]
        return index

    def gather_start(which, stage, value):
        buf, ssem, rsem = gathers[3 * stage : 3 * stage + 3]
        mine = slot_of(groups[stage])
        buf[which, mine] = value
        for k, (where, _) in enumerate(peers(sizes, me, groups[stage])):
            copy = pltpu.make_async_remote_copy(
                src_ref=buf.at[which, mine],
                dst_ref=buf.at[which, mine],
                send_sem=ssem.at[which, k],
                recv_sem=rsem.at[which, mine],
                device_id=where,
                device_id_type=MESH,
            )
            copy.start()
            sent.append(copy)

    def gather_finish(which, stage):
        buf, ssem, rsem = gathers[3 * stage : 3 * stage + 3]
        for k, (where, slot) in enumerate(peers(sizes, me, groups[stage])):
            pltpu.make_async_remote_copy(
                src_ref=buf.at[which, slot],
                dst_ref=buf.at[which, slot],
                send_sem=ssem.at[which, k],
                recv_sem=rsem.at[which, slot],
                device_id=where,
                device_id_type=MESH,
            ).wait_recv()
        return jnp.sum(buf[which], axis=0)

    def rows(d):
        return slice(d * pair, (d + 1) * pair)

    def faces(ref, d):
        return ref[2 * d : 2 * d + 2].reshape(width, columns)

    def keep(ref, d, value):
        ref[2 * d : 2 * d + 2] = value.reshape(2, short, columns)
        return value

    def picks(d):
        row = jnp.concatenate([map_ref[2 * d], map_ref[2 * d + 1] + width], axis=1)
        sign = jnp.concatenate([sign_ref[2 * d], sign_ref[2 * d + 1]], axis=1).astype(jnp.float32)
        place = lax.broadcasted_iota(jnp.int32, (pair, pair), 0)
        return jnp.where(place == row, sign, 0.0)

    def fold(which):
        for d in range(3):
            mid[:, rows(d)] = jnp.dot(
                raw[which, :, rows(d)],
                picks(d).astype(jnp.bfloat16),
                preferred_element_type=jnp.float32,
            ).astype(jnp.bfloat16)
        for d in range(3):
            ops[which, rows(d), :] = jnp.dot(
                picks(d).T.astype(jnp.bfloat16), mid[rows(d), :], preferred_element_type=jnp.float32
            ).astype(jnp.bfloat16)

    def spread(value):
        high = value.astype(jnp.bfloat16).astype(jnp.float32)
        low = value - high
        top, bottom = merge(high, turn(low)), merge(turn(high), low)
        return jnp.concatenate(
            [top[:short], bottom[:short], top[short:], bottom[short:]], axis=0
        ).astype(jnp.bfloat16)

    def dot(block, operand):
        return jnp.dot(block, operand, preferred_element_type=jnp.float32)

    def apply(which, get, out, ready=None):
        near, middle, far = ARRIVAL
        acc[...] = dot(ops[which, :, rows(near)], spread(get(near)))
        acc[...] += dot(ops[which, :, rows(middle)], spread(get(middle)))
        last = spread(get(far))
        for d in reversed(ARRIVAL):
            total = acc[rows(d), :] + dot(ops[which, rows(d), rows(far)], last)
            total = total + turn(total)
            out[2 * d] = merge(total[:short], total[short:width])
            out[2 * d + 1] = merge(total[width : width + short], total[width + short :])
            if ready is not None:
                ready(d)

    def sender(half, exchange, source):
        def ready(d):
            send_face(half, exchange, 2 * d, source)
            send_face(half, exchange, 2 * d + 1, source)

        return ready

    def arrive(half, exchange, d):
        waits[half, exchange, 2 * d].wait_recv()
        waits[half, exchange, 2 * d + 1].wait_recv()
        return faces(got.at[half, exchange], d)

    def fewer(term):
        return jnp.sum(term.reshape(width // 8, 8, columns), axis=0)

    def inner(first, second):
        return sum(fewer(faces(first, d) * faces(second, d)) for d in range(3))

    def message(parts):
        return jnp.concatenate(
            [jnp.sum(part + turn(part), axis=0, keepdims=True) for part in parts], axis=0
        )

    halves = range(2)
    v0, y0, u, y1 = ([own.at[h, k] for h in halves] for k in range(4))
    r0, z0, w0, r1, z1 = ([vec.at[h, k] for h in halves] for k in range(5))

    for h in halves:
        for d in reversed(ARRIVAL):
            sender(h, 0, begin.at[h])(d)
    local[1].wait()
    fold(0)

    for h in halves:
        apply(
            0,
            lambda d: keep(r0[h], d, faces(begin.at[h], d) + arrive(h, 0, d)),
            v0[h],
            sender(h, 1, v0[h]),
        )
    local[2].wait()
    fold(1)
    gamma_parts = [inner(r0[h], v0[h]) for h in halves]

    for h in halves:
        apply(
            1,
            lambda d: keep(z0[h], d, faces(v0[h], d) + arrive(h, 1, d)),
            y0[h],
            sender(h, 2, y0[h]),
        )
    gather_start(0, 0, message(gamma_parts + [inner(z0[h], y0[h]) for h in halves]))
    for stage in range(1, len(groups)):
        gather_start(0, stage, gather_finish(0, stage - 1))

    for h in halves:
        apply(
            0,
            lambda d: keep(w0[h], d, faces(y0[h], d) + arrive(h, 2, d)),
            u[h],
            sender(h, 3, u[h]),
        )
    sums = gather_finish(0, len(groups) - 1)
    gamma0, delta0 = sums[0:2], sums[2:4]
    alpha0 = gamma0 / delta0

    gamma_parts = []
    for h in halves:
        step = alpha0[h : h + 1]
        part = 0.0
        for d in range(3):
            value = keep(r1[h], d, faces(r0[h], d) - step * faces(w0[h], d))
            part = part + fewer(value * (faces(v0[h], d) - step * faces(u[h], d)))
        gamma_parts.append(part)

    def upper(half):
        def ready(d):
            send_face(half, 4, 2 * d + 1, y1[half])

        return ready

    for h in halves:
        apply(
            1,
            lambda d: keep(
                z1[h],
                d,
                faces(z0[h], d) - alpha0[h : h + 1] * (faces(u[h], d) + arrive(h, 3, d)),
            ),
            y1[h],
            None if h else upper(h),
        )
    gather_start(1, 0, message(gamma_parts + [inner(z1[h], y1[h]) for h in halves]))
    for d in reversed(ARRIVAL):
        upper(1)(d)
    for stage in range(1, len(groups)):
        gather_start(1, stage, gather_finish(1, stage - 1))
    sums = gather_finish(1, len(groups) - 1)
    gamma1, delta1 = sums[0:2], sums[2:4]
    beta = gamma1 / gamma0
    alpha1 = gamma1 / (delta1 - beta * gamma1 / alpha0)

    def put(ref, d, first, second):
        ref[d, :short] = merge(first, turn(second))
        ref[d, short:] = merge(turn(first), second)

    def scale(value, h):
        return value[h : h + 1]

    for d in ARRIVAL:
        put(mult_ref, d, *(
            scale(alpha0, h) * z0[h][2 * d]
            + scale(alpha1, h) * (z1[h][2 * d] + scale(beta, h) * z0[h][2 * d])
            for h in halves
        ))
    for d in ARRIVAL:
        for h in halves:
            waits[h, 4, 2 * d].wait_recv()
        put(res_ref, d, *(
            r1[h][2 * d]
            - scale(alpha1, h)
            * (y1[h][2 * d] + got[h, 4, 2 * d] + scale(beta, h) * w0[h][2 * d])
            for h in halves
        ))
    for copy in sent:
        copy.wait_send()


def hand_over(mult_in, res_in, mult_out, res_out, sem):
    copies = [
        pltpu.make_async_copy(mult_in, mult_out, sem.at[0]),
        pltpu.make_async_copy(res_in, res_out, sem.at[1]),
    ]
    for copy in copies:
        copy.start()
    for copy in copies:
        copy.wait()


def shards(sizes, flexibility, stiffness, local_load, face_map, face_sign):
    order = flexibility.shape[-1]
    _, width, columns = local_load.shape[-3:]
    whole = (6, width, columns)
    half = (3, width, columns)
    packed = (6, width // 2, columns)
    dma = pltpu.SemaphoreType.DMA
    scratch = [
        pltpu.VMEM((2, order, order), jnp.bfloat16),
        pltpu.VMEM((order, order), jnp.bfloat16),
        pltpu.VMEM((2, order, order), jnp.bfloat16),
        pltpu.VMEM(whole, jnp.float32),
        pltpu.VMEM((2,) + packed, jnp.float32),
        pltpu.VMEM((2, 4) + packed, jnp.float32),
        pltpu.VMEM((2, 5) + packed, jnp.float32),
        pltpu.VMEM((order, columns), jnp.float32),
        pltpu.VMEM((2, 5) + packed, jnp.float32),
    ]
    scratch += [dma((3,)), dma((2, 5, 6)), dma((2, 5, 6))]
    groups = ((1, 0, 2),) if math.prod(sizes) <= 64 else ((1,), (0,), (2,))
    for group in groups:
        n = math.prod(sizes[d] for d in group)
        scratch += [pltpu.VMEM((2, n, 4, columns), jnp.float32), dma((2, n)), dma((2, n))]
    hbm = pl.BlockSpec(memory_space=pltpu.HBM)
    vmem = pl.BlockSpec(memory_space=pltpu.VMEM)
    multipliers, residual = pl.pallas_call(
        functools.partial(kernel, sizes, groups),
        out_shape=[jax.ShapeDtypeStruct(half, jnp.float32)] * 2,
        in_specs=[hbm, hbm, hbm, vmem, vmem],
        out_specs=[vmem, vmem],
        scratch_shapes=scratch,
        compiler_params=pltpu.CompilerParams(
            collective_id=0, has_side_effects=True, vmem_limit_bytes=60 * 1024 * 1024
        ),
        cost_estimate=pl.CostEstimate(
            flops=16 * order * order * columns, bytes_accessed=4 * order * order, transcendentals=0
        ),
    )(
        stiffness.reshape(order, order),
        flexibility.reshape(order, order),
        local_load.reshape(whole),
        face_map.reshape(6, 1, width),
        face_sign.reshape(6, 1, width),
    )
    multipliers, residual = pl.pallas_call(
        hand_over,
        out_shape=[jax.ShapeDtypeStruct(half, jnp.float32)] * 2,
        in_specs=[vmem, vmem],
        out_specs=[hbm, hbm],
        scratch_shapes=[dma((2,))],
    )(multipliers, residual)
    return multipliers[None, None, None], residual[None, None, None]


def solution(mesh):
    sizes = tuple(mesh.shape[axis] for axis in AXES)
    matrix, face, line = (P(*AXES, *([None] * k)) for k in (2, 3, 2))
    return jax.shard_map(
        functools.partial(shards, sizes),
        mesh=mesh,
        in_specs=(matrix, matrix, face, line, line),
        out_specs=(face, face),
        check_vma=False,
    )
```

time: 38.1 us -> 38.3 us (level)
  no operation moved by 1% of the time
where the time goes in v3:
time: 38.3 us; the launch traced here: 38.1 us
  Pallas kernels  37.4 us (98%)
  between operations  0.64 us (2%)
    pallas_call x1, Pallas kernels, shards(): pl.pallas_call(functools.partial(kernel, sizes, groups), out_shape=[jax.S...  35.7 us
    pallas_call x1, Pallas kernels, shards(): pl.pallas_call(hand_over, out_shape=[jax.ShapeDtypeStruct(half, jnp.float...  1.78 us

profile of v3, /device:TPU:0, one launch (start us, length us, event | category | flops | bytes accessed | tf_op | source)
XLA Modules:
  0.0 38.1 jit_solution(9531647097138097250)
XLA Ops:
  0.6 35.7 %shard_map.68 = (f32[3,128,128]{2,1,0:T(8,128)}, f32[3,128,128]{2,1,0:T(8,128)}) custom-call(bf16[768,768]{1,0:T(8,128)(2,1)} %bitcast.7, bf16[768,768]{1,0:T(8,128)(2,1)} %bitcast.8, f32[6,128,128]{2,1,0:T(8,128)} %bitcast.9, s32[6,1,128]{2,1,0:T(1,128)} %bitcast.12, s32[6,1,128]{2,1,0:T(1,128)} %bitcast.13), custom_call_target="tpu_custom_call" | custom-call | flops 1207959552 | bytes 2359296 | tf_op jit(solution)/shard_map/pallas_call | solution.py:334
  36.3 1.8 %shard_map.69 = (f32[3,128,128]{2,1,0:T(8,128)}, f32[3,128,128]{2,1,0:T(8,128)}) custom-call(f32[3,128,128]{2,1,0:T(8,128)} %get-tuple-element.6.mult_in, f32[3,128,128]{2,1,0:T(8,128)} %get-tuple-element.7.res_in), custom_call_target="tpu_custom_call" | custom-call | tf_op jit(solution)/shard_map/pallas_call | solution.py:353

commit v4 on v2

--- a/solution.py
+++ b/solution.py
@@ -241,17 +241,6 @@
         copy.wait_send()
 
 
-def hand_over(mult_in, res_in, mult_out, res_out, sem):
-    copies = [
-        pltpu.make_async_copy(mult_in, mult_out, sem.at[0]),
-        pltpu.make_async_copy(res_in, res_out, sem.at[1]),
-    ]
-    for copy in copies:
-        copy.start()
-    for copy in copies:
-        copy.wait()
-
-
 def shards(sizes, flexibility, stiffness, local_load, face_map, face_sign):
     order = flexibility.shape[-1]
     _, width, columns = local_load.shape[-3:]
@@ -277,7 +266,7 @@
     vmem = pl.BlockSpec(memory_space=pltpu.VMEM)
     multipliers, residual = pl.pallas_call(
         functools.partial(kernel, sizes, groups),
-        out_shape=[jax.ShapeDtypeStruct(half, jnp.float32)] * 2,
+        out_shape=[pltpu.VMEM(half, jnp.float32)] * 2,
         in_specs=[hbm, hbm, hbm, vmem, vmem],
         out_specs=[vmem, vmem],
         scratch_shapes=scratch,
@@ -294,13 +283,6 @@
         face_map.reshape(6, 1, width),
         face_sign.reshape(6, 1, width),
     )
-    multipliers, residual = pl.pallas_call(
-        hand_over,
-        out_shape=[jax.ShapeDtypeStruct(half, jnp.float32)] * 2,
-        in_specs=[vmem, vmem],
-        out_specs=[hbm, hbm],
-        scratch_shapes=[dma((2,))],
-    )(multipliers, residual)
     return multipliers[None, None, None], residual[None, None, None]
 
 

time: 38.1 us -> 36.9 us (0.969)
  Pallas kernels: 37.2 us -> 34.7 us
  local copies, waits for them, and re-layouts: 0 us -> 1.36 us
    pallas_call x2 -> x1, Pallas kernels: 37.2 us -> 34.7 us  [shards(): pl.pallas_call(functools.partial(kernel, sizes, groups), out_shape=[pltpu...]
    unnamed x0 -> x2, local copies, waits for them, and re-layouts: none -> 1.36 us
where the time goes in v4:
time: 36.9 us; the launch traced here: 36.7 us
  Pallas kernels  34.7 us (94%)
  local copies, waits for them, and re-layouts  1.36 us (4%)
  between operations  0.64 us (2%)
    pallas_call x1, Pallas kernels, shards(): pl.pallas_call(functools.partial(kernel, sizes, groups), out_shape=[pltpu...  34.7 us
    unnamed x2, local copies, waits for them, and re-layouts  1.36 us

profile of v4, /device:TPU:0, one launch (start us, length us, event | category | flops | bytes accessed | tf_op | source)
XLA Modules:
  0.0 36.7 jit_solution(8806851683776537783)
XLA Ops:
  0.6 34.7 %shard_map.68 = (f32[3,128,128]{2,1,0:T(8,128)S(1)}, f32[3,128,128]{2,1,0:T(8,128)S(1)}) custom-call(bf16[768,768]{1,0:T(8,128)(2,1)} %bitcast.9, bf16[768,768]{1,0:T(8,128)(2,1)} %bitcast.10, f32[6,128,128]{2,1,0:T(8,128)} %bitcast.11, s32[6,1,128]{2,1,0:T(1,128)} %bitcast.12, s32[6,1,128]{2,1,0:T(1,128)} %bitcast.13), custom_call_target="tpu_custom_call" | custom-call | flops 1207959552 | bytes 2359296 | tf_op jit(solution)/shard_map/pallas_call | solution.py:267
  35.3 0.7 %copy.9 = f32[1,1,1,3,128,128]{5,4,3,2,1,0:T(8,128)} copy(f32[1,1,1,3,128,128]{5,4,3,2,1,0:T(8,128)S(1)} %bitcast.8) | data formatting | bytes 393216
  36.0 0.7 %copy.10 = f32[1,1,1,3,128,128]{5,4,3,2,1,0:T(8,128)} copy(f32[1,1,1,3,128,128]{5,4,3,2,1,0:T(8,128)S(1)} %bitcast.7) | data formatting | bytes 393216
